TPU v7x, 1024 devices: a whole 8x8x8 slice. The times are simulated.
1024 devices in a mesh: pipe: 32 (over y, z_hi, core), dp: 4 (over z_lo), head: 8 (over x).
Axes of the slice: x: 8, y: 8, z: 8 (z_hi: 2, z_lo: 4; z = z_hi * 4 + z_lo), core: 2. Of those that a mesh axis runs over, the one named last changes fastest.
Arguments:
- activations: bfloat16 [32, 2, 896, 8192], P('pipe', None, 'dp', 'head'), may hold values from -6 to 6
- out_grad: bfloat16 [32, 896, 8192], P('pipe', 'dp', 'head'), may hold values from -1.5 to 1.5
- key_grad: bfloat16 [32, 2, 896, 512], P('pipe', None, 'dp', 'head'), may hold values from -1.5 to 1.5
- key_weight: bfloat16 [32, 8192, 512], P('pipe', 'head'), may hold values from -0.25 to 0.25
- plan: int32 [32, 2], P('pipe'), may hold values from 0 to 1, each once within a row
- first_moment: bfloat16 [32, 8, 1024, 512], P('pipe', 'head', 'dp'), may hold values from -48 to 48
- second_moment: bfloat16 [32, 8, 1024, 512], P('pipe', 'head', 'dp'), may hold values from 10 to 300
Outputs:
- received_grad: bfloat16 [32, 896, 8192], P('pipe', 'dp', 'head')
- new_weight: bfloat16 [32, 8, 1024, 512], P('pipe', 'head', 'dp')
- new_first_moment: bfloat16 [32, 8, 1024, 512], P('pipe', 'head', 'dp')
- new_second_moment: bfloat16 [32, 8, 1024, 512], P('pipe', 'head', 'dp')
- checksum: float32 [32, 8, 4, 512], P('pipe', 'head', 'dp')
Inputs may be any that keep to these rules, and one draw needn't show every extreme that they name: Each row of plan holds 0 and 1 once each.
All inputs are finite; a program needn't handle non-finite values.
Results may differ from a plain program's by a relative error of at most 0.0043.
Values may be sent and summed in bfloat16 or wider, within the bound.
A program may use at most 32 MiB of HBM per device.

v0:
```python
import jax
import jax.numpy as jnp
from jax import lax
from jax.sharding import PartitionSpec as P

beta_one = 0.9
beta_two = 0.95
learn_rate = 0.01
weight_decay = 0.1
epsilon = 1e-08
first_fix = 1.0 - (0.9**10) ** 10
second_fix = 1.0 - (0.95**10) ** 10


def from_behind(value, axis, steps):
    count = lax.axis_size(axis)
    pairs = [(source, (source + steps) % count) for source in range(count)]
    return lax.ppermute(value, axis, pairs)


def send_back(outgoing):
    return from_behind(outgoing, "pipe", -1)


def body(activations, out_grad, key_grad, key_weight, plan, first_moment, second_moment):
    all_keys = lax.all_gather(key_grad[0], "head", axis=2, tiled=True)
    weight = key_weight[0]
    early_keys = lax.dynamic_index_in_dim(all_keys, plan[0, 0], 0, keepdims=False)
    late_keys = lax.dynamic_index_in_dim(all_keys, plan[0, 1], 0, keepdims=False)

    def through(incoming, key_rows):
        added = lax.dot_general(
            key_rows, weight, (((1,), (1,)), ((), ())), preferred_element_type=jnp.float32
        )
        return (incoming.astype(jnp.float32) + added).astype(jnp.bfloat16)

    received = send_back(through(out_grad[0], early_keys))
    passed = send_back(through(received, late_keys))
    shard_rows = first_moment.shape[2]
    row_start = lax.axis_index("dp") * shard_rows
    partial_value = jnp.einsum(
        "mtf,mtc->fc", activations[0], all_keys, preferred_element_type=jnp.float32
    )
    full_gradient = lax.psum(partial_value, "dp")
    gradient = lax.dynamic_slice_in_dim(full_gradient, row_start, shard_rows, 0)
    old_weight = lax.dynamic_slice_in_dim(weight, row_start, shard_rows, 0).astype(jnp.float32)
    first_fresh = beta_one * first_moment[0, 0].astype(jnp.float32) + (1.0 - beta_one) * gradient
    second_fresh = (
        beta_two * second_moment[0, 0].astype(jnp.float32) + (1.0 - beta_two) * gradient * gradient
    )
    update = (
        first_fresh / first_fix / (jnp.sqrt(second_fresh / second_fix) + epsilon)
        + weight_decay * old_weight
    )
    new_weight = (old_weight - learn_rate * update).astype(jnp.bfloat16)
    checksum = jnp.mean(gradient, axis=0)
    return (
        passed[None],
        new_weight[None, None],
        first_fresh.astype(jnp.bfloat16)[None, None],
        second_fresh.astype(jnp.bfloat16)[None, None],
        checksum[None, None, None],
    )


def solution(mesh):
    return jax.shard_map(
        body,
        mesh=mesh,
        in_specs=(
            P("pipe", None, "dp", "head"),
            P("pipe", "dp", "head"),
            P("pipe", None, "dp", "head"),
            P("pipe", "head", None),
            P("pipe", None),
            P("pipe", "head", "dp", None),
            P("pipe", "head", "dp", None),
        ),
        out_specs=(
            P("pipe", "dp", "head"),
            P("pipe", "head", "dp", None),
            P("pipe", "head", "dp", None),
            P("pipe", "head", "dp", None),
            P("pipe", "head", "dp", None),
        ),
        check_vma=False,
    )
```

profile of v0, /device:TPU:1, one launch (start us, length us, event | category | flops | bytes accessed | tf_op | source)
XLA Modules:
  0.0 179.3 jit_solution(8378636443195003681)
XLA Ops:
  7.2 0.0 copy-start
  7.2 0.0 all-reduce.2.cloned.1.call-start
  7.2 1.0 copy.15
  8.2 21.3 %all-gather = bf16[1,2,224,512]{2,1,0,3:T(2,128)(2,1)S(1)} all-gather(bf16[1,2,224,64]{2,1,0,3:T(2,128)(2,1)S(1)} %copy.15), channel_id=2, replica_groups=mesh['pipe'=32,'dp'=4,'head'=8] {'head'}, dimensions={3}, use_global_device_ids=true | all-gather | bytes 516096 | tf_op jit(solution)/shard_map/all_gather | solution.py:26
  29.5 0.4 copy.16
  29.9 0.0 copy-done
  29.9 0.0 copy-start.3
  29.9 0.0 copy-start.1
  29.9 0.0 copy-start.2
  29.9 2.1 %convolution_bitcast_fusion = f32[1024,512]{1,0:T(8,128)} fusion(bf16[1,2,224,1024]{3,2,1,0:T(8,128)(2,1)S(1)} %copy-done, bf16[1,2,224,512]{3,2,1,0:T(8,128)(2,1)S(1)} %copy.16), kind=kOutput, calls=%fused_computation | convolution fusion | flops 469762048 | bytes 3473408 | tf_op jit(solution)/shard_map/mtf,mtc->fc/dot_general | solution.py:41
  32.0 0.0 all-reduce.2.cloned.1.call-update
  32.0 0.0 copy-done.3
  32.0 0.6 fusion.23
  34.6 0.0 copy-done.1
  34.6 0.0 copy-done.2
  34.6 1.3 fusion
  35.8 20.0 %collective-permute-start = (bf16[224,1024]{1,0:T(8,128)(2,1)}, bf16[224,1024]{1,0:T(8,128)(2,1)S(1)}, u32[]{:S(2)}, u32[]{:S(2)}) collective-permute-start(bf16[224,1024]{1,0:T(8,128)(2,1)} %fusion), channel_id=1, source_target_pairs={{0,992},{32,0},{64,32},{96,64},{128,96},{160,128},{192,160},{224,1... | collective-permute-start | bytes 1376264 | tf_op jit(solution)/shard_map/ppermute | solution.py:18
  57.8 7.4 %collective-permute-done = bf16[224,1024]{1,0:T(8,128)(2,1)S(1)} collective-permute-done((bf16[224,1024]{1,0:T(8,128)(2,1)}, bf16[224,1024]{1,0:T(8,128)(2,1)S(1)}, u32[]{:S(2)}, u32[]{:S(2)}) %collective-permute-start) | collective-permute-done | bytes 458784 | tf_op jit(solution)/shard_map/ppermute | solution.py:18
  65.2 0.5 add_convert_fusion
  65.7 1.9 %collective-permute-start.1 = (bf16[224,1024]{1,0:T(8,128)(2,1)S(1)}, bf16[224,1024]{1,0:T(8,128)(2,1)S(1)}, u32[]{:S(2)}, u32[]{:S(2)}) collective-permute-start(bf16[224,1024]{1,0:T(8,128)(2,1)S(1)} %add_convert_fusion), channel_id=1, source_target_pairs={{0,992},{32,0},{64,32},{96,64},{128,96},{160,128},{192,160},{224,1... | collective-permute-start | bytes 1376264 | tf_op jit(solution)/shard_map/ppermute | solution.py:18
  67.6 26.5 %collective-permute-done.1 = bf16[224,1024]{1,0:T(8,128)(2,1)S(1)} collective-permute-done((bf16[224,1024]{1,0:T(8,128)(2,1)S(1)}, bf16[224,1024]{1,0:T(8,128)(2,1)S(1)}, u32[]{:S(2)}, u32[]{:S(2)}) %collective-permute-start.1) | collective-permute-done | bytes 458784 | tf_op jit(solution)/shard_map/ppermute | solution.py:18
  94.2 74.2 %all-reduce.2.cloned.1.call-done = f32[1024,512]{1,0:T(8,128)} async-done(((f32[1024,512]{1,0:T(8,128)}), f32[1024,512]{1,0:T(8,128)}) %all-reduce.2.cloned.1.call-update) | async-done | bytes 2097168 | tf_op jit(solution)/shard_map/psum | solution.py:44
  168.4 2.7 %convert_bitcast_fusion = (bf16[1,1,256,512]{3,2,1,0:T(8,128)(2,1)}, bf16[1,1,256,512]{3,2,1,0:T(8,128)(2,1)}, bf16[1,1,256,512]{3,2,1,0:T(8,128)(2,1)}, f32[512]{0:T(512)S(1)}) fusion(f32[1024,512]{1,0:T(8,128)} %all-reduce.2.cloned.1.call-done, s32[]{:T(128)S(6)} %select_n.13, bf16[1,1,256,512]{3,2,1,0:T(8,128)(2,1)} %param.13, ...), kind=kLoop, calls=%fused_computation.20 | loop fusion | flops 2883072 | bytes 2099204 | tf_op jit(solution)/shard_map/broadcast_in_dim | solution.py:61
  171.1 0.6 broadcast_multiply_fusion
  171.6 0.8 copy.21
Async XLA Ops:
  7.2 22.7 %copy-start = (bf16[1,2,224,1024]{3,2,1,0:T(8,128)(2,1)S(1)}, bf16[1,2,224,1024]{3,2,1,0:T(8,128)(2,1)}, u32[]{:S(2)}) copy-start(bf16[1,2,224,1024]{3,2,1,0:T(8,128)(2,1)} %param.7) | copy-start | bytes 2752516
  7.2 161.2 %all-reduce.2.cloned.1.call-start = ((), (), s32[]{:S(2)}) async-start(), calls=%async_computation | async-start | bytes 4194304 | tf_op jit(solution)/shard_map/psum | solution.py:44
  29.9 2.1 %copy-start.3 = (s32[1,2]{1,0:T(1,128)S(1)}, s32[1,2]{1,0:T(1,128)}, u32[]{:S(2)}) copy-start(s32[1,2]{1,0:T(1,128)} %param.11) | copy-start | bytes 28
  29.9 4.6 %copy-start.1 = (bf16[1,1024,512]{2,1,0:T(8,128)(2,1)S(1)}, bf16[1,1024,512]{2,1,0:T(8,128)(2,1)}, u32[]{:S(2)}) copy-start(bf16[1,1024,512]{2,1,0:T(8,128)(2,1)} %param.10) | copy-start | bytes 3145732
  29.9 4.6 %copy-start.2 = (bf16[1,224,1024]{2,1,0:T(8,128)(2,1)S(1)}, bf16[1,224,1024]{2,1,0:T(8,128)(2,1)}, u32[]{:S(2)}) copy-start(bf16[1,224,1024]{2,1,0:T(8,128)(2,1)} %param.8) | copy-start | bytes 1376260
  35.8 29.4 %collective-permute-start = (bf16[224,1024]{1,0:T(8,128)(2,1)}, bf16[224,1024]{1,0:T(8,128)(2,1)S(1)}, u32[]{:S(2)}, u32[]{:S(2)}) collective-permute-start(bf16[224,1024]{1,0:T(8,128)(2,1)} %fusion), channel_id=1, source_target_pairs={{0,992},{32,0},{64,32},{96,64},{128,96},{160,128},{192,160},{224,1... | collective-permute-start | bytes 1376264 | tf_op jit(solution)/shard_map/ppermute | solution.py:18
  65.7 28.5 %collective-permute-start.1 = (bf16[224,1024]{1,0:T(8,128)(2,1)S(1)}, bf16[224,1024]{1,0:T(8,128)(2,1)S(1)}, u32[]{:S(2)}, u32[]{:S(2)}) collective-permute-start(bf16[224,1024]{1,0:T(8,128)(2,1)S(1)} %add_convert_fusion), channel_id=1, source_target_pairs={{0,992},{32,0},{64,32},{96,64},{128,96},{160,128},{192,160},{224,1... | collective-permute-start | bytes 1376264 | tf_op jit(solution)/shard_map/ppermute | solution.py:18
Sparse Core Ops, SparseCore 0:
  32.1 136.1 all-reduce.1
where the time goes:
time: 180 us; the launch traced here: 179 us
  waiting for transfers between devices  108 us (60%)
  starting transfers between devices  22 us (12%)
  blocking collectives  21.3 us (12%)
  between operations  18 us (10%)
  matrix products  3.79 us (2%)
  other arithmetic  3.26 us (2%)
  local copies, waits for them, and re-layouts  2.75 us (2%)
    psum x1, waiting for transfers between devices, body(): full_gradient = lax.psum(partial_value, 'dp')  74.2 us
    ppermute x2, waiting for transfers between devices, from_behind(): return lax.ppermute(value, axis, pairs)  34 us
    ppermute x2, starting transfers between devices, from_behind(): return lax.ppermute(value, axis, pairs)  21.9 us
    all_gather x1, blocking collectives, body(): all_keys = lax.all_gather(key_grad[0], 'head', axis=2, tiled=True)  21.3 us
  transfers between devices with their start and end apart: 3, of which 3 were waited for; matrix products, arithmetic and copies ran while one was open for 1% of the time, Pallas kernels for 0%

commit v1 on v0

v1 whole, which is shorter than its diff:
```python
import functools

import jax
import jax.numpy as jnp
from jax import lax
from jax.experimental import pallas as pl
from jax.experimental.pallas import tpu as pltpu
from jax.sharding import PartitionSpec as P

MESH = pl.DeviceIdType.MESH
beta_one = 0.9
beta_two = 0.95
learn_rate = 0.01
weight_decay = 0.1
epsilon = 1e-08
first_fix = 1.0 - (0.9**10) ** 10
second_fix = 1.0 - (0.95**10) ** 10

HEADS = 8
N_DP = 4
ROWS = 224
COLS = 512
HEAD_COLS = COLS // HEADS
SHARD = 256
CHUNKS = 4
WIDE = 256
SLAB = 32


def nt(lhs, rhs):
    return lax.dot_general(lhs, rhs, (((1,), (1,)), ((), ())), preferred_element_type=jnp.float32)


def tn(lhs, rhs):
    return lax.dot_general(lhs, rhs, (((0,), (0,)), ((), ())), preferred_element_type=jnp.float32)


def kernel(
    plan, kg, act, og, w, m1, m2,
    out_r, out_w, out_m1, out_m2, out_c,
    kgv, kt, ket, early, late, kn, ke, actv, ogv, wv, m1v, m2v,
    fp, r1, sp, pb, ab, ob, gf, owv, om1v, om2v, ocv,
    load_sem, key_send, key_recv, act_send, act_recv, end_send, end_recv,
    fp_send, fp_recv, sp_send, sp_recv, ob_send, ob_recv, store_sem,
):
    pipe, dp, head = lax.axis_index("pipe"), lax.axis_index("dp"), lax.axis_index("head")
    n_pipe = lax.axis_size("pipe")
    ahead = (lax.rem(pipe + n_pipe - 1, n_pipe), dp, head)
    behind = (lax.rem(pipe + 1, n_pipe), dp, head)
    is_inner = jnp.logical_or(dp == 1, dp == 2)
    is_end = jnp.logical_not(is_inner)
    low = dp < 2
    my_end = jnp.where(low, 0, 3)
    my_inner = jnp.where(low, 1, 2)
    other_inner = jnp.where(low, 2, 1)
    other_end = jnp.where(low, 3, 0)
    even = lax.rem(pipe, 2) == 0

    def peer(step):
        return (pipe, dp, lax.rem(head + step, HEADS))

    def remote(src, dst, send, recv, device):
        return pltpu.make_async_remote_copy(
            src_ref=src, dst_ref=dst, send_sem=send, recv_sem=recv, device_id=device, device_id_type=MESH
        )

    def load(k, src, dst):
        copy = pltpu.make_async_copy(src, dst, load_sem.at[k])
        copy.start()
        return copy

    kg_in = load(0, kg, kgv)
    barrier = pltpu.get_barrier_semaphore()
    greeted = [peer(d) for d in range(1, HEADS)]
    greeted += [(pipe, lax.rem(dp + d, N_DP), head) for d in range(1, N_DP)]
    greeted += [ahead, behind]
    for device in greeted:
        pl.semaphore_signal(barrier, inc=1, device_id=device, device_id_type=MESH)
    act_in = [
        load(1 + 2 * j + m, act.at[m, :, pl.ds(WIDE * j, WIDE)], actv.at[j, pl.ds(ROWS * m, ROWS)])
        for j in range(CHUNKS)
        for m in range(2)
    ]
    w_in = load(9, w, wv)
    og_in = [load(10 + j, og.at[:, pl.ds(WIDE * j, WIDE)], ogv.at[j]) for j in range(CHUNKS)]
    m1_in = load(14, m1, m1v)
    m2_in = load(15, m2, m2v)

    kg_in.wait()
    swap = jnp.full((HEAD_COLS, ROWS), plan[0, 0], jnp.int32) != 0
    zero, one = kgv[0].astype(jnp.float32), kgv[1].astype(jnp.float32)
    kt[0, head] = jnp.where(swap, one, zero).astype(jnp.bfloat16)
    kt[1, head] = jnp.where(swap, zero, one).astype(jnp.bfloat16)
    pl.semaphore_wait(barrier, len(greeted))

    def key_copy(which, d):
        return remote(
            kt.at[which, head], kt.at[which, head], key_send.at[which, d - 1], key_recv.at[which, d - 1], peer(d)
        )

    def end_key_copy(d):
        return remote(ket.at[head], ket.at[head], key_send.at[2, d - 1], key_recv.at[2, d - 1], peer(d))

    order = (4, 3, 5, 2, 6, 1, 7)
    for d in order:
        key_copy(0, d).start()
    for copy in act_in:
        copy.wait()

    targets = (other_end, other_inner, my_inner)
    act_copies = [
        remote(actv.at[targets[k]], ab.at[k], act_send.at[k], act_recv.at[k], (pipe, my_inner, head))
        for k in range(3)
    ]
    end_block = remote(kgv, ket.at[head], end_send, end_recv, (pipe, my_inner, head))

    @pl.when(is_end)
    def _():
        act_copies[0].start()
        end_block.start()

    for d in order:
        key_copy(1, d).start()

    @pl.when(is_end)
    def _():
        act_copies[1].start()
        act_copies[2].start()

    w_in.wait()
    for copy in og_in:
        copy.wait()
    for d in order[::-1]:
        key_copy(0, d).wait_recv()
    early[...] = kt[0].reshape(COLS, ROWS).T

    def fp_copy(j):
        return remote(fp.at[j], r1.at[j], fp_send.at[j], fp_recv.at[j], ahead)

    def sp_copy(j):
        return remote(sp.at[j], out_r.at[:, pl.ds(WIDE * j, WIDE)], sp_send.at[j], sp_recv.at[j], ahead)

    for j in range(CHUNKS):
        added = nt(early[...], wv[WIDE * j : WIDE * (j + 1), :])
        fp[j] = (ogv[j].astype(jnp.float32) + added).astype(jnp.bfloat16)
        fp_copy(j).start()

    @pl.when(is_inner)
    def _():
        end_block.wait_recv()
        for d in order:
            end_key_copy(d).start()

    for d in order[::-1]:
        key_copy(1, d).wait_recv()
    late[...] = kt[1].reshape(COLS, ROWS).T
    swap_all = jnp.full((ROWS, COLS), plan[0, 0], jnp.int32) != 0
    zero, one = early[...].astype(jnp.float32), late[...].astype(jnp.float32)
    kn[:ROWS] = jnp.where(swap_all, one, zero).astype(jnp.bfloat16)
    kn[ROWS:] = jnp.where(swap_all, zero, one).astype(jnp.bfloat16)

    to_end = remote(pb.at[2], ob.at[1], ob_send.at[2], ob_recv.at[1], (pipe, my_end, head))
    to_far = remote(pb.at[0], ob.at[0], ob_send.at[0], ob_recv.at[0], (pipe, other_end, head))
    to_near = remote(pb.at[1], ob.at[0], ob_send.at[1], ob_recv.at[0], (pipe, other_inner, head))

    @pl.when(is_inner)
    def _():
        pb[2] = tn(actv[my_end], kn[...]).astype(jnp.bfloat16)
        to_end.start()

    @pl.when(is_end)
    def _():
        gf[...] = tn(actv[dp], kn[...])

    def second(j):
        fp_copy(j).wait_recv()
        added = nt(late[...], wv[WIDE * j : WIDE * (j + 1), :])
        sp[j] = (r1[j].astype(jnp.float32) + added).astype(jnp.bfloat16)
        sp_copy(j).start()

    @pl.when(even)
    def _():
        for j in range(CHUNKS):
            second(j)

    def pair(k):
        act_copies[k].wait_recv()
        return tn(actv[targets[k]], kn[...]) + tn(ab[k], ke[...])

    @pl.when(is_inner)
    def _():
        for d in order[::-1]:
            end_key_copy(d).wait_recv()
        for m in range(2):
            for h in range(0, HEADS, 2):
                both = jnp.concatenate([ket[h, m], ket[h + 1, m]], axis=0)
                ke[ROWS * m : ROWS * (m + 1), HEAD_COLS * h : HEAD_COLS * (h + 2)] = both.T
        pb[0] = pair(0).astype(jnp.bfloat16)
        to_far.start()
        pb[1] = pair(1).astype(jnp.bfloat16)
        to_near.start()

    @pl.when(jnp.logical_not(even))
    def _():
        for j in range(CHUNKS):
            second(j)

    @pl.when(is_inner)
    def _():
        gf[...] = pair(2)

    m1_in.wait()
    m2_in.wait()
    to_far.wait_recv()

    @pl.when(is_end)
    def _():
        to_end.wait_recv()
        gf[...] = gf[...] + ob[1].astype(jnp.float32)

    def slab(i, total):
        rows = pl.ds(pl.multiple_of(i * SLAB, SLAB), SLAB)
        gradient = gf[rows, :] + ob[0, rows, :].astype(jnp.float32)
        old_weight = wv[pl.ds(pl.multiple_of(dp * SHARD + i * SLAB, SLAB), SLAB), :].astype(jnp.float32)
        first_fresh = beta_one * m1v[rows, :].astype(jnp.float32) + (1.0 - beta_one) * gradient
        second_fresh = beta_two * m2v[rows, :].astype(jnp.float32) + (1.0 - beta_two) * gradient * gradient
        update = (
            first_fresh / first_fix / (jnp.sqrt(second_fresh / second_fix) + epsilon)
            + weight_decay * old_weight
        )
        owv[rows, :] = (old_weight - learn_rate * update).astype(jnp.bfloat16)
        om1v[rows, :] = first_fresh.astype(jnp.bfloat16)
        om2v[rows, :] = second_fresh.astype(jnp.bfloat16)
        return total + jnp.sum(gradient, axis=0, keepdims=True)

    total = lax.fori_loop(0, SHARD // SLAB, slab, jnp.zeros((1, COLS), jnp.float32))
    ocv[...] = total / SHARD
    stores = [(owv, out_w), (om1v, out_m1), (om2v, out_m2), (ocv, out_c)]
    stores = [pltpu.make_async_copy(src, dst, store_sem.at[k]) for k, (src, dst) in enumerate(stores)]
    for copy in stores:
        copy.start()

    for j in range(CHUNKS):
        sp_copy(j).wait_recv()
    for j in range(CHUNKS):
        fp_copy(j).wait_send()
        sp_copy(j).wait_send()
    for d in order:
        key_copy(0, d).wait_send()
        key_copy(1, d).wait_send()

    @pl.when(is_end)
    def _():
        for copy in act_copies:
            copy.wait_send()
        end_block.wait_send()

    @pl.when(is_inner)
    def _():
        for d in order:
            end_key_copy(d).wait_send()
        to_end.wait_send()
        to_far.wait_send()
        to_near.wait_send()

    for copy in stores:
        copy.wait()


def body(activations, out_grad, key_grad, key_weight, plan, first_moment, second_moment):
    keys = jnp.swapaxes(key_grad[0], 1, 2)
    bf16, f32 = jnp.bfloat16, jnp.float32
    vmem = pltpu.VMEM
    dma = pltpu.SemaphoreType.DMA
    shard = jax.ShapeDtypeStruct((SHARD, COLS), bf16)
    anywhere = pl.BlockSpec(memory_space=pl.ANY)
    outs = pl.pallas_call(
        kernel,
        out_shape=(
            jax.ShapeDtypeStruct((ROWS, CHUNKS * WIDE), bf16),
            shard, shard, shard,
            jax.ShapeDtypeStruct((1, COLS), f32),
        ),
        in_specs=[pl.BlockSpec(memory_space=pltpu.SMEM)] + [anywhere] * 6,
        out_specs=[anywhere] * 5,
        scratch_shapes=[
            vmem((2, HEAD_COLS, ROWS), bf16),
            vmem((2, HEADS, HEAD_COLS, ROWS), bf16),
            vmem((HEADS, 2, HEAD_COLS, ROWS), bf16),
            vmem((ROWS, COLS), bf16),
            vmem((ROWS, COLS), bf16),
            vmem((2 * ROWS, COLS), bf16),
            vmem((2 * ROWS, COLS), bf16),
            vmem((CHUNKS, 2 * ROWS, WIDE), bf16),
            vmem((CHUNKS, ROWS, WIDE), bf16),
            vmem((CHUNKS * WIDE, COLS), bf16),
            vmem((SHARD, COLS), bf16),
            vmem((SHARD, COLS), bf16),
            vmem((CHUNKS, ROWS, WIDE), bf16),
            vmem((CHUNKS, ROWS, WIDE), bf16),
            vmem((CHUNKS, ROWS, WIDE), bf16),
            vmem((3, SHARD, COLS), bf16),
            vmem((3, 2 * ROWS, WIDE), bf16),
            vmem((2, SHARD, COLS), bf16),
            vmem((SHARD, COLS), f32),
            vmem((SHARD, COLS), bf16),
            vmem((SHARD, COLS), bf16),
            vmem((SHARD, COLS), bf16),
            vmem((1, COLS), f32),
            dma((16,)),
            dma((3, HEADS - 1)), dma((3, HEADS - 1)),
            dma((3,)), dma((3,)),
            dma, dma,
            dma((CHUNKS,)), dma((CHUNKS,)),
            dma((CHUNKS,)), dma((CHUNKS,)),
            dma((3,)), dma((2,)),
            dma((4,)),
        ],
        compiler_params=pltpu.CompilerParams(
            collective_id=0, has_side_effects=True, vmem_limit_bytes=40 << 20
        ),
        cost_estimate=pl.CostEstimate(flops=1_400_000_000, bytes_accessed=5_000_000, transcendentals=131_072),
    )(plan, keys, activations[0], out_grad[0], key_weight[0], first_moment[0, 0], second_moment[0, 0])
    passed, new_weight, new_first, new_second, checksum = outs
    return passed[None], new_weight[None, None], new_first[None, None], new_second[None, None], checksum[None, None]


def solution(mesh):
    return jax.shard_map(
        body,
        mesh=mesh,
        in_specs=(
            P("pipe", None, "dp", "head"),
            P("pipe", "dp", "head"),
            P("pipe", None, "dp", "head"),
            P("pipe", "head", None),
            P("pipe", None),
            P("pipe", "head", "dp", None),
            P("pipe", "head", "dp", None),
        ),
        out_specs=(
            P("pipe", "dp", "head"),
            P("pipe", "head", "dp", None),
            P("pipe", "head", "dp", None),
            P("pipe", "head", "dp", None),
            P("pipe", "head", "dp", None),
        ),
        check_vma=False,
    )
```

time: 180 us -> 79.2 us (0.44)
  the two profiles are of different devices: /device:TPU:1 before, /device:TPU:128 now
where the time goes in v1:
time: 79.2 us; the launch traced here: 78.8 us
  Pallas kernels  67.9 us (86%)
  local copies, waits for them, and re-layouts  10.3 us (13%)
    pallas_call x1, Pallas kernels, body(): pl.pallas_call(kernel, out_shape=(jax.ShapeDtypeStruct((ROWS, CHUNKS * WI...  67.9 us
    unnamed x19, local copies, waits for them, and re-layouts  10.3 us

profile of v1, /device:TPU:128, one launch (start us, length us, event | category | flops | bytes accessed | tf_op | source)
XLA Modules:
  0.0 78.8 jit_solution(6078480305753693498)
XLA Ops:
  0.6 0.0 copy-start.6
  0.6 0.6 copy-done.6
  1.3 0.0 copy-start
  1.3 1.2 %copy-done = bf16[1,1024,512]{2,1,0:T(8,128)(2,1)S(1)} copy-done((bf16[1,1024,512]{2,1,0:T(8,128)(2,1)S(1)}, bf16[1,1024,512]{2,1,0:T(8,128)(2,1)}, u32[]{:S(2)}) %copy-start) | copy-done | bytes 1048600
  2.5 0.0 copy-start.1
  2.5 1.2 %copy-done.1 = bf16[1,2,224,1024]{3,2,1,0:T(8,128)(2,1)S(1)} copy-done((bf16[1,2,224,1024]{3,2,1,0:T(8,128)(2,1)S(1)}, bf16[1,2,224,1024]{3,2,1,0:T(8,128)(2,1)}, u32[]{:S(2)}) %copy-start.1) | copy-done | bytes 917528
  3.7 0.0 copy-start.2
  3.7 1.0 %copy-done.2 = bf16[1,224,1024]{2,1,0:T(8,128)(2,1)S(1)} copy-done((bf16[1,224,1024]{2,1,0:T(8,128)(2,1)S(1)}, bf16[1,224,1024]{2,1,0:T(8,128)(2,1)}, u32[]{:S(2)}) %copy-start.2) | copy-done | bytes 458776
  4.7 0.0 copy-start.3
  4.7 0.9 %copy-done.3 = bf16[1,1,256,512]{3,2,1,0:T(8,128)(2,1)S(1)} copy-done((bf16[1,1,256,512]{3,2,1,0:T(8,128)(2,1)S(1)}, bf16[1,1,256,512]{3,2,1,0:T(8,128)(2,1)}, u32[]{:S(2)}) %copy-start.3) | copy-done | bytes 262168
  5.7 0.0 copy-start.4
  5.7 0.9 %copy-done.4 = bf16[1,1,256,512]{3,2,1,0:T(8,128)(2,1)S(1)} copy-done((bf16[1,1,256,512]{3,2,1,0:T(8,128)(2,1)S(1)}, bf16[1,1,256,512]{3,2,1,0:T(8,128)(2,1)}, u32[]{:S(2)}) %copy-start.4) | copy-done | bytes 262168
  6.6 0.0 copy-start.5
  6.6 0.8 %copy-done.5 = bf16[1,2,224,64]{2,3,1,0:T(8,128)(2,1)S(1)} copy-done((bf16[1,2,224,64]{2,3,1,0:T(8,128)(2,1)S(1)}, bf16[1,2,224,64]{2,3,1,0:T(8,128)(2,1)}, u32[]{:S(2)}) %copy-start.5) | copy-done | bytes 57368
  7.5 67.9 %shard_map.110 = (bf16[224,1024]{1,0:T(8,128)(2,1)S(1)}, bf16[256,512]{1,0:T(8,128)(2,1)S(1)}, bf16[256,512]{1,0:T(8,128)(2,1)S(1)}, bf16[256,512]{1,0:T(8,128)(2,1)S(1)}, f32[1,512]{1,0:T(1,128)S(1)}) custom-call(s32[1,2]{1,0:T(1,128)S(1)} %copy-done.6, bf16[2,64,224]{2,1,0:T(8,128)(2,1)S(1)} %bitcast.23, bf16[2,224,1024]{2,1,0:T(8,128)(2,1)S(1)} %bitcast.19, ...), custom_call_target="tpu_custom_call" | custom-call | flops 1400000000 | bytes 5000000 | tf_op jit(solution)/shard_map/pallas_call | solution.py:277
  75.4 0.8 copy.17
  76.1 0.7 copy.18
  76.9 0.7 copy.19
  77.6 0.7 copy.20
  78.3 0.6 copy.21
Async XLA Ops:
  0.6 0.7 copy-start.6
  1.3 1.2 %copy-start = (bf16[1,1024,512]{2,1,0:T(8,128)(2,1)S(1)}, bf16[1,1024,512]{2,1,0:T(8,128)(2,1)}, u32[]{:S(2)}) copy-start(bf16[1,1024,512]{2,1,0:T(8,128)(2,1)} %param.10) | copy-start | bytes 3145732
  2.5 1.2 %copy-start.1 = (bf16[1,2,224,1024]{3,2,1,0:T(8,128)(2,1)S(1)}, bf16[1,2,224,1024]{3,2,1,0:T(8,128)(2,1)}, u32[]{:S(2)}) copy-start(bf16[1,2,224,1024]{3,2,1,0:T(8,128)(2,1)} %param.7) | copy-start | bytes 2752516
  3.7 1.0 %copy-start.2 = (bf16[1,224,1024]{2,1,0:T(8,128)(2,1)S(1)}, bf16[1,224,1024]{2,1,0:T(8,128)(2,1)}, u32[]{:S(2)}) copy-start(bf16[1,224,1024]{2,1,0:T(8,128)(2,1)} %param.8) | copy-start | bytes 1376260
  4.7 0.9 %copy-start.3 = (bf16[1,1,256,512]{3,2,1,0:T(8,128)(2,1)S(1)}, bf16[1,1,256,512]{3,2,1,0:T(8,128)(2,1)}, u32[]{:S(2)}) copy-start(bf16[1,1,256,512]{3,2,1,0:T(8,128)(2,1)} %param.12) | copy-start | bytes 786436
  5.7 0.9 %copy-start.4 = (bf16[1,1,256,512]{3,2,1,0:T(8,128)(2,1)S(1)}, bf16[1,1,256,512]{3,2,1,0:T(8,128)(2,1)}, u32[]{:S(2)}) copy-start(bf16[1,1,256,512]{3,2,1,0:T(8,128)(2,1)} %param.13) | copy-start | bytes 786436
  6.6 0.8 %copy-start.5 = (bf16[1,2,224,64]{2,3,1,0:T(8,128)(2,1)S(1)}, bf16[1,2,224,64]{2,3,1,0:T(8,128)(2,1)}, u32[]{:S(2)}) copy-start(bf16[1,2,224,64]{2,3,1,0:T(8,128)(2,1)} %param.9) | copy-start | bytes 172036

commit v2 on v1

--- a/solution.py
+++ b/solution.py
@@ -22,8 +22,10 @@
 COLS = 512
 HEAD_COLS = COLS // HEADS
 SHARD = 256
-CHUNKS = 4
-WIDE = 256
+FEAT = 1024
+TOKEN_PARTS = ((0, 128), (128, 96))
+WIDE = 512
+CHUNKS = [(part, half) for part in range(2) for half in range(2)]
 SLAB = 32
 
 
@@ -38,9 +40,9 @@
 def kernel(
     plan, kg, act, og, w, m1, m2,
     out_r, out_w, out_m1, out_m2, out_c,
-    kgv, kt, ket, early, late, kn, ke, actv, ogv, wv, m1v, m2v,
-    fp, r1, sp, pb, ab, ob, gf, owv, om1v, om2v, ocv,
-    load_sem, key_send, key_recv, act_send, act_recv, end_send, end_recv,
+    kgv, kta, ktb, ktl, ket, early, late, kn, ke, actv, oga, ogb, wv, m1v, m2v,
+    fpa, fpb, r1a, r1b, spa, spb, pb, ab, ob, gf, owv, om1v, om2v, ocv,
+    planv, load_sem, key_send, key_recv, act_send, act_recv, end_send, end_recv,
     fp_send, fp_recv, sp_send, sp_recv, ob_send, ob_recv, store_sem,
 ):
     pipe, dp, head = lax.axis_index("pipe"), lax.axis_index("dp"), lax.axis_index("head")
@@ -69,6 +71,7 @@
         copy.start()
         return copy
 
+    plan_in = load(16, plan, planv)
     kg_in = load(0, kg, kgv)
     barrier = pltpu.get_barrier_semaphore()
     greeted = [peer(d) for d in range(1, HEADS)]
@@ -77,33 +80,55 @@
     for device in greeted:
         pl.semaphore_signal(barrier, inc=1, device_id=device, device_id_type=MESH)
     act_in = [
-        load(1 + 2 * j + m, act.at[m, :, pl.ds(WIDE * j, WIDE)], actv.at[j, pl.ds(ROWS * m, ROWS)])
-        for j in range(CHUNKS)
+        load(1 + 2 * j + m, act.at[m, :, pl.ds(SHARD * j, SHARD)], actv.at[j, pl.ds(ROWS * m, ROWS)])
+        for j in range(N_DP)
         for m in range(2)
     ]
     w_in = load(9, w, wv)
-    og_in = [load(10 + j, og.at[:, pl.ds(WIDE * j, WIDE)], ogv.at[j]) for j in range(CHUNKS)]
+    ogv, fp, r1, sp = (oga, ogb), (fpa, fpb), (r1a, r1b), (spa, spb)
+    og_in = [
+        load(10 + j, og.at[pl.ds(*TOKEN_PARTS[part]), pl.ds(WIDE * half, WIDE)], ogv[part].at[half])
+        for j, (part, half) in enumerate(CHUNKS)
+    ]
     m1_in = load(14, m1, m1v)
     m2_in = load(15, m2, m2v)
 
+    plan_in.wait()
     kg_in.wait()
-    swap = jnp.full((HEAD_COLS, ROWS), plan[0, 0], jnp.int32) != 0
+    swap = jnp.full((HEAD_COLS, ROWS), planv[0, 0], jnp.int32) != 0
     zero, one = kgv[0].astype(jnp.float32), kgv[1].astype(jnp.float32)
-    kt[0, head] = jnp.where(swap, one, zero).astype(jnp.bfloat16)
-    kt[1, head] = jnp.where(swap, zero, one).astype(jnp.bfloat16)
+    first = jnp.where(swap, one, zero).astype(jnp.bfloat16)
+    kta[head] = first[:, : TOKEN_PARTS[0][1]]
+    ktb[head] = first[:, TOKEN_PARTS[0][1] :]
+    ktl[head] = jnp.where(swap, zero, one).astype(jnp.bfloat16)
     pl.semaphore_wait(barrier, len(greeted))
 
-    def key_copy(which, d):
-        return remote(
-            kt.at[which, head], kt.at[which, head], key_send.at[which, d - 1], key_recv.at[which, d - 1], peer(d)
-        )
+    early_parts = (kta, ktb)
+
+    def early_copy(part, d):
+        block = early_parts[part].at[head]
+        return remote(block, block, key_send.at[part, d - 1], key_recv.at[part, d - 1], peer(d))
+
+    def passed_on(blocks, row, d, via_below):
+        if d in (1, 2, 6, 7):
+            owner, device = head, peer(d)
+        elif d == 3 or (d == 4 and via_below):
+            owner, device = lax.rem(head + HEADS - 2, HEADS), peer(d - 2)
+        else:
+            owner, device = lax.rem(head + 2, HEADS), peer(d + 2)
+        block = blocks.at[owner]
+        return remote(block, block, key_send.at[row, d - 1], key_recv.at[row, d - 1], device)
+
+    def late_copy(d):
+        return passed_on(ktl, 2, d, True)
 
     def end_key_copy(d):
-        return remote(ket.at[head], ket.at[head], key_send.at[2, d - 1], key_recv.at[2, d - 1], peer(d))
-
-    order = (4, 3, 5, 2, 6, 1, 7)
-    for d in order:
-        key_copy(0, d).start()
+        return passed_on(ket, 3, d, False)
+
+    far, near = (4, 3, 5, 2, 6, 1, 7), (2, 6, 1, 7)
+    for part in range(2):
+        for d in far:
+            early_copy(part, d).start()
     for copy in act_in:
         copy.wait()
 
@@ -116,45 +141,64 @@
 
     @pl.when(is_end)
     def _():
+        end_block.start()
         act_copies[0].start()
-        end_block.start()
-
-    for d in order:
-        key_copy(1, d).start()
-
-    @pl.when(is_end)
-    def _():
-        act_copies[1].start()
-        act_copies[2].start()
+
+    for d in near:
+        late_copy(d).start()
+
+    def fp_copy(j):
+        part, half = CHUNKS[j]
+        return remote(fp[part].at[half], r1[part].at[half], fp_send.at[j], fp_recv.at[j], ahead)
+
+    def sp_copy(j):
+        part, half = CHUNKS[j]
+        place = out_r.at[pl.ds(*TOKEN_PARTS[part]), pl.ds(WIDE * half, WIDE)]
+        return remote(sp[part].at[half], place, sp_send.at[j], sp_recv.at[j], ahead)
+
+    def first(j):
+        part, half = CHUNKS[j]
+        start, rows = TOKEN_PARTS[part]
+        added = nt(early[start : start + rows, :], wv[WIDE * half : WIDE * (half + 1), :])
+        fp[part][half] = (ogv[part][half].astype(jnp.float32) + added).astype(jnp.bfloat16)
+        fp_copy(j).start()
 
     w_in.wait()
     for copy in og_in:
         copy.wait()
-    for d in order[::-1]:
-        key_copy(0, d).wait_recv()
-    early[...] = kt[0].reshape(COLS, ROWS).T
-
-    def fp_copy(j):
-        return remote(fp.at[j], r1.at[j], fp_send.at[j], fp_recv.at[j], ahead)
-
-    def sp_copy(j):
-        return remote(sp.at[j], out_r.at[:, pl.ds(WIDE * j, WIDE)], sp_send.at[j], sp_recv.at[j], ahead)
-
-    for j in range(CHUNKS):
-        added = nt(early[...], wv[WIDE * j : WIDE * (j + 1), :])
-        fp[j] = (ogv[j].astype(jnp.float32) + added).astype(jnp.bfloat16)
-        fp_copy(j).start()
+    for part, (start, rows) in enumerate(TOKEN_PARTS):
+        for d in far[::-1]:
+            early_copy(part, d).wait_recv()
+        early[start : start + rows, :] = early_parts[part][...].reshape(COLS, rows).T
+        for j in range(len(CHUNKS)):
+            if CHUNKS[j][0] == part:
+                first(j)
+        if part == 0:
+
+            @pl.when(is_inner)
+            def _():
+                end_block.wait_recv()
+                for d in near:
+                    end_key_copy(d).start()
+
+    late_copy(2).wait_recv()
+    late_copy(3).start()
+    late_copy(4).start()
+    late_copy(6).wait_recv()
+    late_copy(5).start()
 
     @pl.when(is_inner)
     def _():
-        end_block.wait_recv()
-        for d in order:
-            end_key_copy(d).start()
-
-    for d in order[::-1]:
-        key_copy(1, d).wait_recv()
-    late[...] = kt[1].reshape(COLS, ROWS).T
-    swap_all = jnp.full((ROWS, COLS), plan[0, 0], jnp.int32) != 0
+        end_key_copy(2).wait_recv()
+        end_key_copy(3).start()
+        end_key_copy(6).wait_recv()
+        end_key_copy(4).start()
+        end_key_copy(5).start()
+
+    for d in (1, 7, 5, 3, 4):
+        late_copy(d).wait_recv()
+    late[...] = ktl[...].reshape(COLS, ROWS).T
+    swap_all = jnp.full((ROWS, COLS), planv[0, 0], jnp.int32) != 0
     zero, one = early[...].astype(jnp.float32), late[...].astype(jnp.float32)
     kn[:ROWS] = jnp.where(swap_all, one, zero).astype(jnp.bfloat16)
     kn[ROWS:] = jnp.where(swap_all, zero, one).astype(jnp.bfloat16)
@@ -163,6 +207,23 @@
     to_far = remote(pb.at[0], ob.at[0], ob_send.at[0], ob_recv.at[0], (pipe, other_end, head))
     to_near = remote(pb.at[1], ob.at[0], ob_send.at[1], ob_recv.at[0], (pipe, other_inner, head))
 
+    def second(j):
+        part, half = CHUNKS[j]
+        start, rows = TOKEN_PARTS[part]
+        fp_copy(j).wait_recv()
+        added = nt(late[start : start + rows, :], wv[WIDE * half : WIDE * (half + 1), :])
+        sp[part][half] = (r1[part][half].astype(jnp.float32) + added).astype(jnp.bfloat16)
+        sp_copy(j).start()
+
+    @pl.when(is_end)
+    def _():
+        act_copies[1].start()
+
+    @pl.when(even)
+    def _():
+        for j in range(len(CHUNKS)):
+            second(j)
+
     @pl.when(is_inner)
     def _():
         pb[2] = tn(actv[my_end], kn[...]).astype(jnp.bfloat16)
@@ -171,17 +232,6 @@
     @pl.when(is_end)
     def _():
         gf[...] = tn(actv[dp], kn[...])
-
-    def second(j):
-        fp_copy(j).wait_recv()
-        added = nt(late[...], wv[WIDE * j : WIDE * (j + 1), :])
-        sp[j] = (r1[j].astype(jnp.float32) + added).astype(jnp.bfloat16)
-        sp_copy(j).start()
-
-    @pl.when(even)
-    def _():
-        for j in range(CHUNKS):
-            second(j)
 
     def pair(k):
         act_copies[k].wait_recv()
@@ -189,7 +239,7 @@
 
     @pl.when(is_inner)
     def _():
-        for d in order[::-1]:
+        for d in (1, 7, 3, 5, 4):
             end_key_copy(d).wait_recv()
         for m in range(2):
             for h in range(0, HEADS, 2):
@@ -197,16 +247,21 @@
                 ke[ROWS * m : ROWS * (m + 1), HEAD_COLS * h : HEAD_COLS * (h + 2)] = both.T
         pb[0] = pair(0).astype(jnp.bfloat16)
         to_far.start()
+
+    @pl.when(jnp.logical_not(even))
+    def _():
+        for j in range(len(CHUNKS)):
+            second(j)
+
+    @pl.when(is_end)
+    def _():
+        act_copies[1].wait_send()
+        act_copies[2].start()
+
+    @pl.when(is_inner)
+    def _():
         pb[1] = pair(1).astype(jnp.bfloat16)
         to_near.start()
-
-    @pl.when(jnp.logical_not(even))
-    def _():
-        for j in range(CHUNKS):
-            second(j)
-
-    @pl.when(is_inner)
-    def _():
         gf[...] = pair(2)
 
     m1_in.wait()
@@ -240,30 +295,41 @@
     for copy in stores:
         copy.start()
 
-    for j in range(CHUNKS):
+    for j in range(len(CHUNKS)):
         sp_copy(j).wait_recv()
-    for j in range(CHUNKS):
+    for j in range(len(CHUNKS)):
         fp_copy(j).wait_send()
         sp_copy(j).wait_send()
-    for d in order:
-        key_copy(0, d).wait_send()
-        key_copy(1, d).wait_send()
-
-    @pl.when(is_end)
-    def _():
-        for copy in act_copies:
-            copy.wait_send()
+    for d in far:
+        early_copy(0, d).wait_send()
+        early_copy(1, d).wait_send()
+        late_copy(d).wait_send()
+
+    @pl.when(is_end)
+    def _():
+        act_copies[0].wait_send()
+        act_copies[2].wait_send()
         end_block.wait_send()
 
     @pl.when(is_inner)
     def _():
-        for d in order:
+        for d in far:
             end_key_copy(d).wait_send()
         to_end.wait_send()
         to_far.wait_send()
         to_near.wait_send()
 
     for copy in stores:
+        copy.wait()
+
+
+def hand_over(*refs):
+    count = (len(refs) - 1) // 2
+    sems = refs[-1]
+    copies = [pltpu.make_async_copy(refs[k], refs[count + k], sems.at[k]) for k in range(count)]
+    for copy in copies:
+        copy.start()
+    for copy in copies:
         copy.wait()
 
 
@@ -274,45 +340,53 @@
     dma = pltpu.SemaphoreType.DMA
     shard = jax.ShapeDtypeStruct((SHARD, COLS), bf16)
     anywhere = pl.BlockSpec(memory_space=pl.ANY)
+    hbm = pl.BlockSpec(memory_space=pltpu.HBM)
     outs = pl.pallas_call(
         kernel,
         out_shape=(
-            jax.ShapeDtypeStruct((ROWS, CHUNKS * WIDE), bf16),
+            jax.ShapeDtypeStruct((ROWS, FEAT), bf16),
             shard, shard, shard,
             jax.ShapeDtypeStruct((1, COLS), f32),
         ),
-        in_specs=[pl.BlockSpec(memory_space=pltpu.SMEM)] + [anywhere] * 6,
+        in_specs=[hbm] * 7,
         out_specs=[anywhere] * 5,
         scratch_shapes=[
             vmem((2, HEAD_COLS, ROWS), bf16),
-            vmem((2, HEADS, HEAD_COLS, ROWS), bf16),
+            vmem((HEADS, HEAD_COLS, TOKEN_PARTS[0][1]), bf16),
+            vmem((HEADS, HEAD_COLS, TOKEN_PARTS[1][1]), bf16),
+            vmem((HEADS, HEAD_COLS, ROWS), bf16),
             vmem((HEADS, 2, HEAD_COLS, ROWS), bf16),
             vmem((ROWS, COLS), bf16),
             vmem((ROWS, COLS), bf16),
             vmem((2 * ROWS, COLS), bf16),
             vmem((2 * ROWS, COLS), bf16),
-            vmem((CHUNKS, 2 * ROWS, WIDE), bf16),
-            vmem((CHUNKS, ROWS, WIDE), bf16),
-            vmem((CHUNKS * WIDE, COLS), bf16),
+            vmem((N_DP, 2 * ROWS, SHARD), bf16),
+            vmem((2, TOKEN_PARTS[0][1], WIDE), bf16),
+            vmem((2, TOKEN_PARTS[1][1], WIDE), bf16),
+            vmem((FEAT, COLS), bf16),
             vmem((SHARD, COLS), bf16),
             vmem((SHARD, COLS), bf16),
-            vmem((CHUNKS, ROWS, WIDE), bf16),
-            vmem((CHUNKS, ROWS, WIDE), bf16),
-            vmem((CHUNKS, ROWS, WIDE), bf16),
+            vmem((2, TOKEN_PARTS[0][1], WIDE), bf16),
+            vmem((2, TOKEN_PARTS[1][1], WIDE), bf16),
+            vmem((2, TOKEN_PARTS[0][1], WIDE), bf16),
+            vmem((2, TOKEN_PARTS[1][1], WIDE), bf16),
+            vmem((2, TOKEN_PARTS[0][1], WIDE), bf16),
+            vmem((2, TOKEN_PARTS[1][1], WIDE), bf16),
             vmem((3, SHARD, COLS), bf16),
-            vmem((3, 2 * ROWS, WIDE), bf16),
+            vmem((3, 2 * ROWS, SHARD), bf16),
             vmem((2, SHARD, COLS), bf16),
             vmem((SHARD, COLS), f32),
             vmem((SHARD, COLS), bf16),
             vmem((SHARD, COLS), bf16),
             vmem((SHARD, COLS), bf16),
             vmem((1, COLS), f32),
-            dma((16,)),
-            dma((3, HEADS - 1)), dma((3, HEADS - 1)),
+            pltpu.SMEM((1, 2), jnp.int32),
+            dma((17,)),
+            dma((4, HEADS - 1)), dma((4, HEADS - 1)),
             dma((3,)), dma((3,)),
             dma, dma,
-            dma((CHUNKS,)), dma((CHUNKS,)),
-            dma((CHUNKS,)), dma((CHUNKS,)),
+            dma((len(CHUNKS),)), dma((len(CHUNKS),)),
+            dma((len(CHUNKS),)), dma((len(CHUNKS),)),
             dma((3,)), dma((2,)),
             dma((4,)),
         ],
@@ -320,7 +394,15 @@
             collective_id=0, has_side_effects=True, vmem_limit_bytes=40 << 20
         ),
         cost_estimate=pl.CostEstimate(flops=1_400_000_000, bytes_accessed=5_000_000, transcendentals=131_072),
-    )(plan, keys, activations[0], out_grad[0], key_weight[0], first_moment[0, 0], second_moment[0, 0])
+    )(*[pltpu.with_memory_space_constraint(v, pltpu.HBM) for v in (plan, keys, activations[0], out_grad[0], key_weight[0], first_moment[0, 0], second_moment[0, 0])])
+    outs = pl.pallas_call(
+        hand_over,
+        out_shape=tuple(jax.ShapeDtypeStruct(value.shape, value.dtype) for value in outs),
+        in_specs=[anywhere] * len(outs),
+        out_specs=[hbm] * len(outs),
+        scratch_shapes=[dma((len(outs),))],
+        compiler_params=pltpu.CompilerParams(vmem_limit_bytes=1 << 20),
+    )(*outs)
     passed, new_weight, new_first, new_second, checksum = outs
     return passed[None], new_weight[None, None], new_first[None, None], new_second[None, None], checksum[None, None]
 

time: 79.2 us -> 64.3 us (0.81)
  the two profiles are of different devices: /device:TPU:128 before, /device:TPU:177 now
where the time goes in v2:
time: 64.3 us; the launch traced here: 64.1 us
  Pallas kernels  63.4 us (99%)
    pallas_call x1, Pallas kernels, body(): pl.pallas_call(kernel, out_shape=(jax.ShapeDtypeStruct((ROWS, FEAT), bf16...  62.4 us

profile of v2, /device:TPU:177, one launch (start us, length us, event | category | flops | bytes accessed | tf_op | source)
XLA Modules:
  0.0 64.1 jit_solution(18141847014031773709)
XLA Ops:
  0.6 62.4 %shard_map.110 = (bf16[224,1024]{1,0:T(8,128)(2,1)S(1)}, bf16[256,512]{1,0:T(8,128)(2,1)S(1)}, bf16[256,512]{1,0:T(8,128)(2,1)S(1)}, bf16[256,512]{1,0:T(8,128)(2,1)S(1)}, f32[1,512]{1,0:T(1,128)S(1)}) custom-call(s32[1,2]{1,0:T(1,128)} %plan.1, bf16[2,64,224]{2,1,0:T(8,128)(2,1)} %bitcast.22, bf16[2,224,1024]{2,1,0:T(8,128)(2,1)} %bitcast.14, ...), custom_call_target="tpu_custom_call" | custom-call | flops 1400000000 | bytes 5000000 | tf_op jit(solution)/shard_map/pallas_call | solution.py:344
  63.0 1.1 %shard_map.111 = (bf16[224,1024]{1,0:T(8,128)(2,1)}, bf16[256,512]{1,0:T(8,128)(2,1)}, bf16[256,512]{1,0:T(8,128)(2,1)}, bf16[256,512]{1,0:T(8,128)(2,1)}, f32[1,512]{1,0:T(1,128)}) custom-call(bf16[224,1024]{1,0:T(8,128)(2,1)S(1)} %get-tuple-element.15.refs_0_, bf16[256,512]{1,0:T(8,128)(2,1)S(1)} %get-tuple-element.16.refs_1_, ...), custom_call_target="tpu_custom_call" | custom-call | tf_op jit(solution)/shard_map/pallas_call | solution.py:398

commit v3 on v2

--- a/solution.py
+++ b/solution.py
@@ -41,7 +41,7 @@
     plan, kg, act, og, w, m1, m2,
     out_r, out_w, out_m1, out_m2, out_c,
     kgv, kta, ktb, ktl, ket, early, late, kn, ke, actv, oga, ogb, wv, m1v, m2v,
-    fpa, fpb, r1a, r1b, spa, spb, pb, ab, ob, gf, owv, om1v, om2v, ocv,
+    fpa, fpb, r1a, r1b, spa, spb, pb, ab, own, ob, gf, owv, om1v, om2v, ocv,
     planv, load_sem, key_send, key_recv, act_send, act_recv, end_send, end_recv,
     fp_send, fp_recv, sp_send, sp_recv, ob_send, ob_recv, store_sem,
 ):
@@ -181,6 +181,10 @@
                 for d in near:
                     end_key_copy(d).start()
 
+    @pl.when(is_end)
+    def _():
+        act_copies[1].start()
+
     late_copy(2).wait_recv()
     late_copy(3).start()
     late_copy(4).start()
@@ -215,10 +219,6 @@
         sp[part][half] = (r1[part][half].astype(jnp.float32) + added).astype(jnp.bfloat16)
         sp_copy(j).start()
 
-    @pl.when(is_end)
-    def _():
-        act_copies[1].start()
-
     @pl.when(even)
     def _():
         for j in range(len(CHUNKS)):
@@ -235,10 +235,12 @@
 
     def pair(k):
         act_copies[k].wait_recv()
-        return tn(actv[targets[k]], kn[...]) + tn(ab[k], ke[...])
+        return own[k] + tn(ab[k], ke[...])
 
     @pl.when(is_inner)
     def _():
+        for k in range(3):
+            own[k] = tn(actv[targets[k]], kn[...])
         for d in (1, 7, 3, 5, 4):
             end_key_copy(d).wait_recv()
         for m in range(2):
@@ -374,6 +376,7 @@
             vmem((2, TOKEN_PARTS[1][1], WIDE), bf16),
             vmem((3, SHARD, COLS), bf16),
             vmem((3, 2 * ROWS, SHARD), bf16),
+            vmem((3, SHARD, COLS), f32),
             vmem((2, SHARD, COLS), bf16),
             vmem((SHARD, COLS), f32),
             vmem((SHARD, COLS), bf16),

time: 64.3 us -> 64.2 us (level)
  no operation moved by 1% of the time
where the time goes in v3:
time: 64.2 us; the launch traced here: 63.9 us
  Pallas kernels  63.3 us (99%)
    pallas_call x1, Pallas kernels, body(): pl.pallas_call(kernel, out_shape=(jax.ShapeDtypeStruct((ROWS, FEAT), bf16...  62.2 us

profile of v3, /device:TPU:177, one launch (start us, length us, event | category | flops | bytes accessed | tf_op | source)
XLA Modules:
  0.0 63.9 jit_solution(103547547731249751)
XLA Ops:
  0.6 62.2 %shard_map.110 = (bf16[224,1024]{1,0:T(8,128)(2,1)S(1)}, bf16[256,512]{1,0:T(8,128)(2,1)S(1)}, bf16[256,512]{1,0:T(8,128)(2,1)S(1)}, bf16[256,512]{1,0:T(8,128)(2,1)S(1)}, f32[1,512]{1,0:T(1,128)S(1)}) custom-call(s32[1,2]{1,0:T(1,128)} %plan.1, bf16[2,64,224]{2,1,0:T(8,128)(2,1)} %bitcast.22, bf16[2,224,1024]{2,1,0:T(8,128)(2,1)} %bitcast.14, ...), custom_call_target="tpu_custom_call" | custom-call | flops 1400000000 | bytes 5000000 | tf_op jit(solution)/shard_map/pallas_call | solution.py:346
  62.8 1.1 %shard_map.111 = (bf16[224,1024]{1,0:T(8,128)(2,1)}, bf16[256,512]{1,0:T(8,128)(2,1)}, bf16[256,512]{1,0:T(8,128)(2,1)}, bf16[256,512]{1,0:T(8,128)(2,1)}, f32[1,512]{1,0:T(1,128)}) custom-call(bf16[224,1024]{1,0:T(8,128)(2,1)S(1)} %get-tuple-element.15.refs_0_, bf16[256,512]{1,0:T(8,128)(2,1)S(1)} %get-tuple-element.16.refs_1_, ...), custom_call_target="tpu_custom_call" | custom-call | tf_op jit(solution)/shard_map/pallas_call | solution.py:401

commit v4 on v2

--- a/solution.py
+++ b/solution.py
@@ -219,6 +219,10 @@
     def _():
         act_copies[1].start()
 
+    @pl.when(jnp.logical_and(is_end, even))
+    def _():
+        act_copies[2].start()
+
     @pl.when(even)
     def _():
         for j in range(len(CHUNKS)):
@@ -253,7 +257,7 @@
         for j in range(len(CHUNKS)):
             second(j)
 
-    @pl.when(is_end)
+    @pl.when(jnp.logical_and(is_end, jnp.logical_not(even)))
     def _():
         act_copies[1].wait_send()
         act_copies[2].start()
@@ -308,6 +312,11 @@
     @pl.when(is_end)
     def _():
         act_copies[0].wait_send()
+
+        @pl.when(even)
+        def _():
+            act_copies[1].wait_send()
+
         act_copies[2].wait_send()
         end_block.wait_send()
 

time: 64.3 us -> 64.3 us (level)
  no operation moved by 1% of the time
where the time goes in v4:
time: 64.3 us; the launch traced here: 64.1 us
  Pallas kernels  63.5 us (99%)
    pallas_call x1, Pallas kernels, body(): pl.pallas_call(kernel, out_shape=(jax.ShapeDtypeStruct((ROWS, FEAT), bf16...  62.4 us

profile of v4, /device:TPU:177, one launch (start us, length us, event | category | flops | bytes accessed | tf_op | source)
XLA Modules:
  0.0 64.1 jit_solution(11093260102295622035)
XLA Ops:
  0.6 62.4 %shard_map.110 = (bf16[224,1024]{1,0:T(8,128)(2,1)S(1)}, bf16[256,512]{1,0:T(8,128)(2,1)S(1)}, bf16[256,512]{1,0:T(8,128)(2,1)S(1)}, bf16[256,512]{1,0:T(8,128)(2,1)S(1)}, f32[1,512]{1,0:T(1,128)S(1)}) custom-call(s32[1,2]{1,0:T(1,128)} %plan.1, bf16[2,64,224]{2,1,0:T(8,128)(2,1)} %bitcast.22, bf16[2,224,1024]{2,1,0:T(8,128)(2,1)} %bitcast.14, ...), custom_call_target="tpu_custom_call" | custom-call | flops 1400000000 | bytes 5000000 | tf_op jit(solution)/shard_map/pallas_call | solution.py:353
  63.0 1.1 %shard_map.111 = (bf16[224,1024]{1,0:T(8,128)(2,1)}, bf16[256,512]{1,0:T(8,128)(2,1)}, bf16[256,512]{1,0:T(8,128)(2,1)}, bf16[256,512]{1,0:T(8,128)(2,1)}, f32[1,512]{1,0:T(1,128)}) custom-call(bf16[224,1024]{1,0:T(8,128)(2,1)S(1)} %get-tuple-element.15.refs_0_, bf16[256,512]{1,0:T(8,128)(2,1)S(1)} %get-tuple-element.16.refs_1_, ...), custom_call_target="tpu_custom_call" | custom-call | tf_op jit(solution)/shard_map/pallas_call | solution.py:407
